TPU v7x, 32 devices: a whole 2x2x4 slice. The times are simulated.
32 devices in a mesh: groups: 2 (over y), set: 4 (over x, core), gy: 4 (over z).
Axes of the slice: x: 2, y: 2, z: 4, core: 2. Of those that a mesh axis runs over, the one named last changes fastest.
Arguments:
- grain_ids: int32 [16, 64, 128], P('groups', 'gy'), parts along dimension 0, may hold values from 0 to 1023, as said below
- colouring: int32 [2048], P('groups'), parts along dimension 0, may hold values from 0 to 15
- mobility: float32 [16, 64, 128], P('groups', 'gy'), parts along dimension 0, may hold values from 0.5 to 2
Outputs:
- level: float32 [32, 8, 64, 128], P(('groups', 'set'), None, 'gy'), parts along dimension 0
There are 2 independent parts, one for each index of `groups`. A program takes and returns all parts, laid end to end along the dimension named above; each array names one. Nothing has to cross between parts.
Inputs may be any that keep to these rules, and one draw needn't show every extreme that they name: `grain_ids`: each cell holds the number of the cube of 4 x 4 x 4 cells in which it lies after each of its coordinates is moved by -1, 0 or 1 cell with periodic wrap; cubes are numbered with z slowest and x fastest.
All inputs are finite; a program needn't handle non-finite values.
Results may differ from a plain program's by a relative error of at most 0.0003.
Values sent between devices are 32-bit elements; how exact they have to be, the bound alone decides.
A program may use at most 64 MiB of HBM per device.

v0:
```python
from functools import partial

import jax
import jax.numpy as jnp
from jax import lax
from jax.sharding import PartitionSpec as P

SETS = 16
STEPS = 2
REINIT = 3


TIME_STEP = 0.08
PSEUDO_STEP = 0.3
WENO_EPS = 1e-06


def padded_2(shard, sides, width):
    for axis, dim in sides:
        count, length = (lax.axis_size(axis), shard.shape[dim])
        up = [(i, (i + 1) % count) for i in range(count)]
        down = [(j, i) for i, j in up]
        last = lax.slice_in_dim(shard, length - width, length, axis=dim)
        leading = lax.slice_in_dim(shard, 0, width, axis=dim)
        before = lax.ppermute(last, axis, up)
        after = lax.ppermute(leading, axis, down)
        shard = jnp.concatenate([before, shard, after], axis=dim)
    return shard


def joined(shard, axis, combine):
    everything = jax.tree.map(lambda part: lax.all_gather(part, axis), shard)
    leading = jax.tree.map(lambda part: part[0], everything)

    def step(k, so_far):
        return combine(so_far, jax.tree.map(lambda part: part[k], everything))

    return lax.fori_loop(1, lax.axis_size(axis), step, leading)


def squared(value):
    return value * value


def weno_side(diffs):
    far_left, near_left, middle, near_right, far_right = diffs
    smooth_one = 13.0 / 12.0 * squared(far_left - 2.0 * near_left + middle) + 0.25 * squared(
        far_left - 4.0 * near_left + 3.0 * middle
    )
    smooth_two = 13.0 / 12.0 * squared(near_left - 2.0 * middle + near_right) + 0.25 * squared(
        near_left - near_right
    )
    smooth_three = 13.0 / 12.0 * squared(middle - 2.0 * near_right + far_right) + 0.25 * squared(
        3.0 * middle - 4.0 * near_right + far_right
    )
    alpha_one = 0.1 / squared(WENO_EPS + smooth_one)
    alpha_two = 0.6 / squared(WENO_EPS + smooth_two)
    alpha_three = 0.3 / squared(WENO_EPS + smooth_three)
    weight_sum = alpha_one + alpha_two + alpha_three
    guess_one = far_left / 3.0 - 7.0 * near_left / 6.0 + 11.0 * middle / 6.0
    guess_two = -near_left / 6.0 + 5.0 * middle / 6.0 + near_right / 3.0
    guess_three = middle / 3.0 + 5.0 * near_right / 6.0 - far_right / 6.0
    return (alpha_one * guess_one + alpha_two * guess_two + alpha_three * guess_three) / weight_sum


def one_sided(fetch_at):
    values = [fetch_at(offset) for offset in range(-3, 4)]
    backward = [values[position + 1] - values[position] for position in range(6)]
    minus_side = weno_side(backward[0:5])
    plus_side = weno_side([backward[5], backward[4], backward[3], backward[2], backward[1]])
    return (minus_side, plus_side)


def godunov(minus_side, plus_side, signum):
    growing = jnp.maximum(
        squared(jnp.maximum(minus_side, 0.0)), squared(jnp.minimum(plus_side, 0.0))
    )
    shrinking = jnp.maximum(
        squared(jnp.minimum(minus_side, 0.0)), squared(jnp.maximum(plus_side, 0.0))
    )
    return jnp.where(signum > 0.0, growing, shrinking)


def rolled(field, along_axis, offset):
    return jnp.roll(field, -offset, along_axis)


def sliced(padded, offset):
    return padded[:, :, 3 + offset : padded.shape[2] - 3 + offset]


def settle(padded, signum):
    center = padded[:, :, 3:-3]
    gradient = jnp.zeros_like(center)
    minus_side, plus_side = one_sided(partial(rolled, center, 1))
    gradient = gradient + godunov(minus_side, plus_side, signum)
    minus_side, plus_side = one_sided(partial(sliced, padded))
    gradient = gradient + godunov(minus_side, plus_side, signum)
    minus_side, plus_side = one_sided(partial(rolled, center, 3))
    gradient = gradient + godunov(minus_side, plus_side, signum)
    return center - PSEUDO_STEP * signum * (jnp.sqrt(gradient) - 1.0)


def local_ranks(level):
    lowest = level[0]
    second = jnp.full_like(lowest, jnp.inf)
    for position in range(1, level.shape[0]):
        second = jnp.minimum(second, jnp.maximum(lowest, level[position]))
        lowest = jnp.minimum(lowest, level[position])
    return (lowest, second)


def pair_min(left_pair, right_pair):
    lowest = jnp.minimum(left_pair[0], right_pair[0])
    second = jnp.minimum(
        jnp.maximum(left_pair[0], right_pair[0]), jnp.minimum(left_pair[1], right_pair[1])
    )
    return (lowest, second)


def project(level, lowest, second):
    other = jnp.where(level == lowest[None], second[None], lowest[None])
    return 0.5 * (level - other)


def shards(grain_ids, colouring, mobility):
    local_count = SETS // lax.axis_size("set")
    first_set = lax.axis_index("set") * local_count
    colour_cell = jnp.take(colouring, grain_ids)
    set_index = first_set + jnp.arange(local_count, dtype=jnp.int32)[:, None, None, None]
    level = jnp.where(colour_cell[None] == set_index, -0.5, 0.5).astype(jnp.float32)
    for outer_step in range(STEPS):
        padded = padded_2(level, (("gy", 2),), 1)
        laplace = jnp.roll(level, 1, 1) + jnp.roll(level, -1, 1)
        laplace = laplace + padded[:, :, 2:] + padded[:, :, :-2]
        laplace = laplace + jnp.roll(level, 1, 3) + jnp.roll(level, -1, 3) - 6.0 * level
        level = level + TIME_STEP * mobility[None] * laplace
        lowest, second = local_ranks(level)
        lowest, second = joined((lowest, second), "set", pair_min)
        level = project(level, lowest, second)
        signum = level / jnp.sqrt(level * level + 1.0)
        for sweep in range(REINIT):
            padded = padded_2(level, (("gy", 2),), 3)
            level = settle(padded, signum)
    return level


def solution(mesh):
    placed = (P("groups", "gy", None), P("groups"), P("groups", "gy", None))
    return jax.shard_map(
        shards,
        mesh=mesh,
        in_specs=placed,
        out_specs=P(("groups", "set"), None, "gy", None),
        check_vma=False,
    )
```

profile of v0, /device:TPU:0, one launch (start us, length us, event | category | flops | bytes accessed | tf_op | source)
XLA Modules:
  0.0 184.8 jit_solution(893538229288036633)
XLA Ops:
  0.9 65.3 %gather_fusion = s32[16384]{0:T(1024)S(1)} fusion(s32[1024]{0:T(1024)S(1)} %copy-done, s32[16384]{0:T(1024)S(1)} %broadcast_clamp_fusion), kind=kCustom, calls=%fused_computation | custom fusion | bytes 196608 | tf_op jit(solution)/shard_map/jit(_take)/gather | solution.py:129
  66.3 5.1 %collective-permute-start = (f32[4,8,1,128]{3,2,1,0:T(1,128)S(1)}, f32[4,8,1,128]{3,2,1,0:T(1,128)S(1)}, u32[]{:S(2)}, u32[]{:S(2)}) collective-permute-start(f32[4,8,1,128]{3,2,1,0:T(1,128)S(1)} %get-tuple-element.477), channel_id=1, source_target_pairs={{1,0},{2,1},{3,2},{0,3},{5,4},{6,5},{7,6},{4,7},{9,8},{10,9},{11,1... | collective-permute-start | bytes 49160 | tf_op jit(solution)/shard_map/ppermute | solution.py:26
  72.9 4.1 %collective-permute-done.1 = f32[4,8,1,128]{3,2,1,0:T(1,128)S(1)} collective-permute-done((f32[4,8,1,128]{3,2,1,0:T(1,128)S(1)}, f32[4,8,1,128]{3,2,1,0:T(1,128)S(1)}, u32[]{:S(2)}, u32[]{:S(2)}) %collective-permute-start.1) | collective-permute-done | bytes 16416 | tf_op jit(solution)/shard_map/ppermute | solution.py:25
  77.3 5.8 %all_gather.17 = f32[4,8,16,128]{3,2,1,0:T(8,128)S(1)} all-gather(f32[1,8,16,128]{3,2,1,0:T(8,128)S(1)} %get-tuple-element.467), channel_id=1, replica_groups=mesh['groups'=2,'set'=4,'gy'=4] {'set'}, dimensions={0}, use_global_device_ids=true | all-gather | bytes 327680 | tf_op jit(solution)/shard_map/all_gather | solution.py:32
  83.1 5.8 %all_gather.16 = f32[4,8,16,128]{3,2,1,0:T(8,128)S(1)} all-gather(f32[1,8,16,128]{3,2,1,0:T(8,128)S(1)} %get-tuple-element.468), channel_id=1, replica_groups=mesh['groups'=2,'set'=4,'gy'=4] {'set'}, dimensions={0}, use_global_device_ids=true | all-gather | bytes 327680 | tf_op jit(solution)/shard_map/all_gather | solution.py:32
  90.3 3.8 %collective-permute-start.3 = (f32[4,8,3,128]{3,2,1,0:T(4,128)S(1)}, f32[4,8,3,128]{3,2,1,0:T(4,128)S(1)}, u32[]{:S(2)}, u32[]{:S(2)}) collective-permute-start(f32[4,8,3,128]{3,2,1,0:T(4,128)S(1)} %get-tuple-element.454), channel_id=1, source_target_pairs={{1,0},{2,1},{3,2},{0,3},{5,4},{6,5},{7,6},{4,7},{9,8},{10,9},{11,1... | collective-permute-start | bytes 147464 | tf_op jit(solution)/shard_map/ppermute | solution.py:26
  94.1 2.9 %collective-permute-done.2 = f32[4,8,3,128]{3,2,1,0:T(4,128)S(1)} collective-permute-done((f32[4,8,3,128]{3,2,1,0:T(4,128)S(1)}, f32[4,8,3,128]{3,2,1,0:T(4,128)S(1)}, u32[]{:S(2)}, u32[]{:S(2)}) %collective-permute-start.2) | collective-permute-done | bytes 49184 | tf_op jit(solution)/shard_map/ppermute | solution.py:25
  97.0 4.6 %multiply_subtract_fusion.5 = f32[4,8,16,128]{3,2,1,0:T(8,128)S(1)} fusion(f32[4,8,16,128]{3,2,1,0:T(8,128)S(1)} %subtract_multiply_fusion.31, f32[4,8,16,3]{3,2,1,0:T(8,128)S(1)} %get-tuple-element.464, f32[4,8,16,125]{3,2,1,0:T(8,128)S(1)} %get-tuple-element.466, f32[4,8,16,2]{3,2,1,0:T(8,128)S(1)} %get-tuple-element.456, ...), kind=kLoop, calls=%fused_computation.546 | loop fusion | flops 29556736 | bytes 3768320 | tf_op jit(solution)/shard_map/sub | solution.py:101
  102.6 3.8 %collective-permute-start.5 = (f32[4,8,3,128]{3,2,1,0:T(4,128)S(1)}, f32[4,8,3,128]{3,2,1,0:T(4,128)S(1)}, u32[]{:S(2)}, u32[]{:S(2)}) collective-permute-start(f32[4,8,3,128]{3,2,1,0:T(4,128)S(1)} %get-tuple-element.428), channel_id=1, source_target_pairs={{1,0},{2,1},{3,2},{0,3},{5,4},{6,5},{7,6},{4,7},{9,8},{10,9},{11,1... | collective-permute-start | bytes 147464 | tf_op jit(solution)/shard_map/ppermute | solution.py:26
  108.8 4.9 %multiply_subtract_fusion.4 = f32[4,8,16,128]{3,2,1,0:T(8,128)S(1)} fusion(f32[4,8,16,128]{3,2,1,0:T(8,128)S(1)} %multiply_subtract_fusion.5, f32[4,8,16,3]{3,2,1,0:T(8,128)S(1)} %get-tuple-element.438, f32[4,8,16,125]{3,2,1,0:T(8,128)S(1)} %get-tuple-element.440, f32[4,8,16,2]{3,2,1,0:T(8,128)S(1)} %get-tuple-element.430, ...), kind=kLoop, calls=%fused_computation.479 | loop fusion | flops 29818880 | bytes 4161536 | tf_op jit(solution)/shard_map/sub | solution.py:101
  115.9 2.7 %collective-permute-start.7 = (f32[4,8,3,128]{3,2,1,0:T(4,128)S(1)}, f32[4,8,3,128]{3,2,1,0:T(4,128)S(1)}, u32[]{:S(2)}, u32[]{:S(2)}) collective-permute-start(f32[4,8,3,128]{3,2,1,0:T(4,128)S(1)} %get-tuple-element.402), channel_id=1, source_target_pairs={{1,0},{2,1},{3,2},{0,3},{5,4},{6,5},{7,6},{4,7},{9,8},{10,9},{11,1... | collective-permute-start | bytes 147464 | tf_op jit(solution)/shard_map/ppermute | solution.py:26
  120.9 4.9 %multiply_subtract_fusion.3 = f32[4,8,16,128]{3,2,1,0:T(8,128)S(1)} fusion(f32[4,8,16,128]{3,2,1,0:T(8,128)S(1)} %multiply_subtract_fusion.4, f32[4,8,16,3]{3,2,1,0:T(8,128)S(1)} %get-tuple-element.412, f32[4,8,16,125]{3,2,1,0:T(8,128)S(1)} %get-tuple-element.414, f32[4,8,16,2]{3,2,1,0:T(8,128)S(1)} %get-tuple-element.404, ...), kind=kLoop, calls=%fused_computation.412 | loop fusion | flops 29818880 | bytes 4161536 | tf_op jit(solution)/shard_map/sub | solution.py:101
  126.2 3.9 %collective-permute-start.8 = (f32[4,8,1,128]{3,2,1,0:T(1,128)S(1)}, f32[4,8,1,128]{3,2,1,0:T(1,128)S(1)}, u32[]{:S(2)}, u32[]{:S(2)}) collective-permute-start(f32[4,8,1,128]{3,2,1,0:T(1,128)S(1)} %get-tuple-element.387), channel_id=1, source_target_pairs={{1,0},{2,1},{3,2},{0,3},{5,4},{6,5},{7,6},{4,7},{9,8},{10,9},{11,1... | collective-permute-start | bytes 49160 | tf_op jit(solution)/shard_map/ppermute | solution.py:26
  131.5 4.1 %collective-permute-done.9 = f32[4,8,1,128]{3,2,1,0:T(1,128)S(1)} collective-permute-done((f32[4,8,1,128]{3,2,1,0:T(1,128)S(1)}, f32[4,8,1,128]{3,2,1,0:T(1,128)S(1)}, u32[]{:S(2)}, u32[]{:S(2)}) %collective-permute-start.9) | collective-permute-done | bytes 16416 | tf_op jit(solution)/shard_map/ppermute | solution.py:25
  135.9 5.8 %all_gather.19 = f32[4,8,16,128]{3,2,1,0:T(8,128)S(1)} all-gather(f32[1,8,16,128]{3,2,1,0:T(8,128)S(1)} %get-tuple-element.377), channel_id=1, replica_groups=mesh['groups'=2,'set'=4,'gy'=4] {'set'}, dimensions={0}, use_global_device_ids=true | all-gather | bytes 327680 | tf_op jit(solution)/shard_map/all_gather | solution.py:32
  141.7 5.8 %all_gather.18 = f32[4,8,16,128]{3,2,1,0:T(8,128)S(1)} all-gather(f32[1,8,16,128]{3,2,1,0:T(8,128)S(1)} %get-tuple-element.378), channel_id=1, replica_groups=mesh['groups'=2,'set'=4,'gy'=4] {'set'}, dimensions={0}, use_global_device_ids=true | all-gather | bytes 327680 | tf_op jit(solution)/shard_map/all_gather | solution.py:32
  148.9 3.8 %collective-permute-start.11 = (f32[4,8,3,128]{3,2,1,0:T(4,128)S(1)}, f32[4,8,3,128]{3,2,1,0:T(4,128)S(1)}, u32[]{:S(2)}, u32[]{:S(2)}) collective-permute-start(f32[4,8,3,128]{3,2,1,0:T(4,128)S(1)} %get-tuple-element.364), channel_id=1, source_target_pairs={{1,0},{2,1},{3,2},{0,3},{5,4},{6,5},{7,6},{4,7},{9,8},{10,9},{11,1... | collective-permute-start | bytes 147464 | tf_op jit(solution)/shard_map/ppermute | solution.py:26
  152.7 2.9 %collective-permute-done.10 = f32[4,8,3,128]{3,2,1,0:T(4,128)S(1)} collective-permute-done((f32[4,8,3,128]{3,2,1,0:T(4,128)S(1)}, f32[4,8,3,128]{3,2,1,0:T(4,128)S(1)}, u32[]{:S(2)}, u32[]{:S(2)}) %collective-permute-start.10) | collective-permute-done | bytes 49184 | tf_op jit(solution)/shard_map/ppermute | solution.py:25
  155.6 4.6 %multiply_subtract_fusion.2 = f32[4,8,16,128]{3,2,1,0:T(8,128)S(1)} fusion(f32[4,8,16,128]{3,2,1,0:T(8,128)S(1)} %subtract_multiply_fusion.15, f32[4,8,16,3]{3,2,1,0:T(8,128)S(1)} %get-tuple-element.374, f32[4,8,16,125]{3,2,1,0:T(8,128)S(1)} %get-tuple-element.376, f32[4,8,16,2]{3,2,1,0:T(8,128)S(1)} %get-tuple-element.366, ...), kind=kLoop, calls=%fused_computation.343 | loop fusion | flops 29556736 | bytes 3768320 | tf_op jit(solution)/shard_map/sub | solution.py:101
  161.3 3.8 %collective-permute-start.13 = (f32[4,8,3,128]{3,2,1,0:T(4,128)S(1)}, f32[4,8,3,128]{3,2,1,0:T(4,128)S(1)}, u32[]{:S(2)}, u32[]{:S(2)}) collective-permute-start(f32[4,8,3,128]{3,2,1,0:T(4,128)S(1)} %get-tuple-element.338), channel_id=1, source_target_pairs={{1,0},{2,1},{3,2},{0,3},{5,4},{6,5},{7,6},{4,7},{9,8},{10,9},{11,1... | collective-permute-start | bytes 147464 | tf_op jit(solution)/shard_map/ppermute | solution.py:26
  165.1 2.3 %collective-permute-done.12 = f32[4,8,3,128]{3,2,1,0:T(4,128)S(1)} collective-permute-done((f32[4,8,3,128]{3,2,1,0:T(4,128)S(1)}, f32[4,8,3,128]{3,2,1,0:T(4,128)S(1)}, u32[]{:S(2)}, u32[]{:S(2)}) %collective-permute-start.12) | collective-permute-done | bytes 49184 | tf_op jit(solution)/shard_map/ppermute | solution.py:25
  167.4 4.9 %multiply_subtract_fusion.1 = f32[4,8,16,128]{3,2,1,0:T(8,128)S(1)} fusion(f32[4,8,16,128]{3,2,1,0:T(8,128)S(1)} %multiply_subtract_fusion.2, f32[4,8,16,3]{3,2,1,0:T(8,128)S(1)} %get-tuple-element.348, f32[4,8,16,125]{3,2,1,0:T(8,128)S(1)} %get-tuple-element.350, f32[4,8,16,2]{3,2,1,0:T(8,128)S(1)} %get-tuple-element.340, ...), kind=kLoop, calls=%fused_computation.276 | loop fusion | flops 29818880 | bytes 4161536 | tf_op jit(solution)/shard_map/sub | solution.py:101
  174.5 2.7 %collective-permute-start.15 = (f32[4,8,3,128]{3,2,1,0:T(4,128)S(1)}, f32[4,8,3,128]{3,2,1,0:T(4,128)S(1)}, u32[]{:S(2)}, u32[]{:S(2)}) collective-permute-start(f32[4,8,3,128]{3,2,1,0:T(4,128)S(1)} %get-tuple-element.312), channel_id=1, source_target_pairs={{1,0},{2,1},{3,2},{0,3},{5,4},{6,5},{7,6},{4,7},{9,8},{10,9},{11,1... | collective-permute-start | bytes 147464 | tf_op jit(solution)/shard_map/ppermute | solution.py:26
  179.5 5.3 %multiply_subtract_fusion = f32[4,8,16,128]{3,2,1,0:T(8,128)} fusion(f32[4,8,16,128]{3,2,1,0:T(8,128)S(1)} %multiply_subtract_fusion.1, f32[4,8,16,3]{3,2,1,0:T(8,128)S(1)} %get-tuple-element.322, f32[4,8,16,125]{3,2,1,0:T(8,128)S(1)} %get-tuple-element.324, f32[4,8,16,2]{3,2,1,0:T(8,128)S(1)} %get-tuple-element.314, ...), kind=kLoop, calls=%fused_computation.209 | loop fusion | flops 29818880 | bytes 4161536 | tf_op jit(solution)/shard_map/sub | solution.py:101
  (137 shorter events, 20.5 us)
Async XLA Ops:
  0.0 0.9 copy-start
  0.9 65.3 %copy-start.1 = (s32[8,16,128]{2,1,0:T(8,128)S(1)}, s32[8,16,128]{2,1,0:T(8,128)}, u32[]{:S(2)}) copy-start(s32[8,16,128]{2,1,0:T(8,128)} %param.7) | copy-start | bytes 196612
  66.3 6.5 %collective-permute-start = (f32[4,8,1,128]{3,2,1,0:T(1,128)S(1)}, f32[4,8,1,128]{3,2,1,0:T(1,128)S(1)}, u32[]{:S(2)}, u32[]{:S(2)}) collective-permute-start(f32[4,8,1,128]{3,2,1,0:T(1,128)S(1)} %get-tuple-element.477), channel_id=1, source_target_pairs={{1,0},{2,1},{3,2},{0,3},{5,4},{6,5},{7,6},{4,7},{9,8},{10,9},{11,1... | collective-permute-start | bytes 49160 | tf_op jit(solution)/shard_map/ppermute | solution.py:26
  71.5 5.5 %collective-permute-start.1 = (f32[4,8,1,128]{3,2,1,0:T(1,128)S(1)}, f32[4,8,1,128]{3,2,1,0:T(1,128)S(1)}, u32[]{:S(2)}, u32[]{:S(2)}) collective-permute-start(f32[4,8,1,128]{3,2,1,0:T(1,128)S(1)} %get-tuple-element.478), channel_id=1, source_target_pairs={{0,1},{1,2},{2,3},{3,0},{4,5},{5,6},{6,7},{7,4},{8,9},{9,10},{10,1... | collective-permute-start | bytes 49160 | tf_op jit(solution)/shard_map/ppermute | solution.py:25
  71.7 0.8 copy-start.2
  90.2 6.8 %collective-permute-start.2 = (f32[4,8,3,128]{3,2,1,0:T(4,128)S(1)}, f32[4,8,3,128]{3,2,1,0:T(4,128)S(1)}, u32[]{:S(2)}, u32[]{:S(2)}) collective-permute-start(f32[4,8,3,128]{3,2,1,0:T(4,128)S(1)} %get-tuple-element.453), channel_id=1, source_target_pairs={{0,1},{1,2},{2,3},{3,0},{4,5},{5,6},{6,7},{7,4},{8,9},{9,10},{10,1... | collective-permute-start | bytes 147464 | tf_op jit(solution)/shard_map/ppermute | solution.py:25
  90.3 6.7 %collective-permute-start.3 = (f32[4,8,3,128]{3,2,1,0:T(4,128)S(1)}, f32[4,8,3,128]{3,2,1,0:T(4,128)S(1)}, u32[]{:S(2)}, u32[]{:S(2)}) collective-permute-start(f32[4,8,3,128]{3,2,1,0:T(4,128)S(1)} %get-tuple-element.454), channel_id=1, source_target_pairs={{1,0},{2,1},{3,2},{0,3},{5,4},{6,5},{7,6},{4,7},{9,8},{10,9},{11,1... | collective-permute-start | bytes 147464 | tf_op jit(solution)/shard_map/ppermute | solution.py:26
  102.6 6.2 %collective-permute-start.4 = (f32[4,8,3,128]{3,2,1,0:T(4,128)S(1)}, f32[4,8,3,128]{3,2,1,0:T(4,128)S(1)}, u32[]{:S(2)}, u32[]{:S(2)}) collective-permute-start(f32[4,8,3,128]{3,2,1,0:T(4,128)S(1)} %get-tuple-element.427), channel_id=1, source_target_pairs={{0,1},{1,2},{2,3},{3,0},{4,5},{5,6},{6,7},{7,4},{8,9},{9,10},{10,1... | collective-permute-start | bytes 147464 | tf_op jit(solution)/shard_map/ppermute | solution.py:25
  102.6 6.2 %collective-permute-start.5 = (f32[4,8,3,128]{3,2,1,0:T(4,128)S(1)}, f32[4,8,3,128]{3,2,1,0:T(4,128)S(1)}, u32[]{:S(2)}, u32[]{:S(2)}) collective-permute-start(f32[4,8,3,128]{3,2,1,0:T(4,128)S(1)} %get-tuple-element.428), channel_id=1, source_target_pairs={{1,0},{2,1},{3,2},{0,3},{5,4},{6,5},{7,6},{4,7},{9,8},{10,9},{11,1... | collective-permute-start | bytes 147464 | tf_op jit(solution)/shard_map/ppermute | solution.py:26
  114.8 6.1 %collective-permute-start.6 = (f32[4,8,3,128]{3,2,1,0:T(4,128)S(1)}, f32[4,8,3,128]{3,2,1,0:T(4,128)S(1)}, u32[]{:S(2)}, u32[]{:S(2)}) collective-permute-start(f32[4,8,3,128]{3,2,1,0:T(4,128)S(1)} %get-tuple-element.401), channel_id=1, source_target_pairs={{0,1},{1,2},{2,3},{3,0},{4,5},{5,6},{6,7},{7,4},{8,9},{9,10},{10,1... | collective-permute-start | bytes 147464 | tf_op jit(solution)/shard_map/ppermute | solution.py:25
  115.9 5.0 %collective-permute-start.7 = (f32[4,8,3,128]{3,2,1,0:T(4,128)S(1)}, f32[4,8,3,128]{3,2,1,0:T(4,128)S(1)}, u32[]{:S(2)}, u32[]{:S(2)}) collective-permute-start(f32[4,8,3,128]{3,2,1,0:T(4,128)S(1)} %get-tuple-element.402), channel_id=1, source_target_pairs={{1,0},{2,1},{3,2},{0,3},{5,4},{6,5},{7,6},{4,7},{9,8},{10,9},{11,1... | collective-permute-start | bytes 147464 | tf_op jit(solution)/shard_map/ppermute | solution.py:26
  126.2 5.3 %collective-permute-start.8 = (f32[4,8,1,128]{3,2,1,0:T(1,128)S(1)}, f32[4,8,1,128]{3,2,1,0:T(1,128)S(1)}, u32[]{:S(2)}, u32[]{:S(2)}) collective-permute-start(f32[4,8,1,128]{3,2,1,0:T(1,128)S(1)} %get-tuple-element.387), channel_id=1, source_target_pairs={{1,0},{2,1},{3,2},{0,3},{5,4},{6,5},{7,6},{4,7},{9,8},{10,9},{11,1... | collective-permute-start | bytes 49160 | tf_op jit(solution)/shard_map/ppermute | solution.py:26
  130.0 5.5 %collective-permute-start.9 = (f32[4,8,1,128]{3,2,1,0:T(1,128)S(1)}, f32[4,8,1,128]{3,2,1,0:T(1,128)S(1)}, u32[]{:S(2)}, u32[]{:S(2)}) collective-permute-start(f32[4,8,1,128]{3,2,1,0:T(1,128)S(1)} %get-tuple-element.388), channel_id=1, source_target_pairs={{0,1},{1,2},{2,3},{3,0},{4,5},{5,6},{6,7},{7,4},{8,9},{9,10},{10,1... | collective-permute-start | bytes 49160 | tf_op jit(solution)/shard_map/ppermute | solution.py:25
  148.8 6.8 %collective-permute-start.10 = (f32[4,8,3,128]{3,2,1,0:T(4,128)S(1)}, f32[4,8,3,128]{3,2,1,0:T(4,128)S(1)}, u32[]{:S(2)}, u32[]{:S(2)}) collective-permute-start(f32[4,8,3,128]{3,2,1,0:T(4,128)S(1)} %get-tuple-element.363), channel_id=1, source_target_pairs={{0,1},{1,2},{2,3},{3,0},{4,5},{5,6},{6,7},{7,4},{8,9},{9,10},{10,1... | collective-permute-start | bytes 147464 | tf_op jit(solution)/shard_map/ppermute | solution.py:25
  148.9 6.7 %collective-permute-start.11 = (f32[4,8,3,128]{3,2,1,0:T(4,128)S(1)}, f32[4,8,3,128]{3,2,1,0:T(4,128)S(1)}, u32[]{:S(2)}, u32[]{:S(2)}) collective-permute-start(f32[4,8,3,128]{3,2,1,0:T(4,128)S(1)} %get-tuple-element.364), channel_id=1, source_target_pairs={{1,0},{2,1},{3,2},{0,3},{5,4},{6,5},{7,6},{4,7},{9,8},{10,9},{11,1... | collective-permute-start | bytes 147464 | tf_op jit(solution)/shard_map/ppermute | solution.py:26
  161.2 6.2 %collective-permute-start.12 = (f32[4,8,3,128]{3,2,1,0:T(4,128)S(1)}, f32[4,8,3,128]{3,2,1,0:T(4,128)S(1)}, u32[]{:S(2)}, u32[]{:S(2)}) collective-permute-start(f32[4,8,3,128]{3,2,1,0:T(4,128)S(1)} %get-tuple-element.337), channel_id=1, source_target_pairs={{0,1},{1,2},{2,3},{3,0},{4,5},{5,6},{6,7},{7,4},{8,9},{9,10},{10,1... | collective-permute-start | bytes 147464 | tf_op jit(solution)/shard_map/ppermute | solution.py:25
  161.3 6.2 %collective-permute-start.13 = (f32[4,8,3,128]{3,2,1,0:T(4,128)S(1)}, f32[4,8,3,128]{3,2,1,0:T(4,128)S(1)}, u32[]{:S(2)}, u32[]{:S(2)}) collective-permute-start(f32[4,8,3,128]{3,2,1,0:T(4,128)S(1)} %get-tuple-element.338), channel_id=1, source_target_pairs={{1,0},{2,1},{3,2},{0,3},{5,4},{6,5},{7,6},{4,7},{9,8},{10,9},{11,1... | collective-permute-start | bytes 147464 | tf_op jit(solution)/shard_map/ppermute | solution.py:26
  173.4 6.1 %collective-permute-start.14 = (f32[4,8,3,128]{3,2,1,0:T(4,128)S(1)}, f32[4,8,3,128]{3,2,1,0:T(4,128)S(1)}, u32[]{:S(2)}, u32[]{:S(2)}) collective-permute-start(f32[4,8,3,128]{3,2,1,0:T(4,128)S(1)} %get-tuple-element.311), channel_id=1, source_target_pairs={{0,1},{1,2},{2,3},{3,0},{4,5},{5,6},{6,7},{7,4},{8,9},{9,10},{10,1... | collective-permute-start | bytes 147464 | tf_op jit(solution)/shard_map/ppermute | solution.py:25
  174.5 5.0 %collective-permute-start.15 = (f32[4,8,3,128]{3,2,1,0:T(4,128)S(1)}, f32[4,8,3,128]{3,2,1,0:T(4,128)S(1)}, u32[]{:S(2)}, u32[]{:S(2)}) collective-permute-start(f32[4,8,3,128]{3,2,1,0:T(4,128)S(1)} %get-tuple-element.312), channel_id=1, source_target_pairs={{1,0},{2,1},{3,2},{0,3},{5,4},{6,5},{7,6},{4,7},{9,8},{10,9},{11,1... | collective-permute-start | bytes 147464 | tf_op jit(solution)/shard_map/ppermute | solution.py:26
where the time goes:
time: 185 us
  local copies, waits for them, and re-layouts  72.5 us (39%)
  starting transfers between devices  32.2 us (17%)
  other arithmetic  31.1 us (17%)
  waiting for transfers between devices  24.9 us (13%)
  blocking collectives  23.3 us (13%)
    gather x1, local copies, waits for them, and re-layouts, shards(): colour_cell = jnp.take(colouring, grain_ids)  65.3 us
    ppermute x8, starting transfers between devices, padded_2(): after = lax.ppermute(leading, axis, down)  29.7 us
    sub x6, other arithmetic, settle(): return center - PSEUDO_STEP * signum * (jnp.sqrt(gradient) - 1.0)  29.2 us
    all_gather x4, blocking collectives, joined(): everything = jax.tree.map(lambda part: lax.all_gather(part, axis), shard)  23.3 us
    ppermute x8, waiting for transfers between devices, padded_2(): before = lax.ppermute(last, axis, up)  23.1 us
    slice x72, local copies, waits for them, and re-layouts, rolled(): return jnp.roll(field, -offset, along_axis)  5.55 us
  transfers between devices with their start and end apart: 16, of which 10 were waited for; matrix products, arithmetic and copies ran while one was open for 0% of the time, Pallas kernels for 0%

commit v1 on v0

v1 whole, which is shorter than its diff:
```python
import functools

import jax
import jax.numpy as jnp
from jax import lax
from jax.experimental import pallas as pl
from jax.experimental.pallas import tpu as pltpu
from jax.sharding import PartitionSpec as P

SETS = 16
REINIT = 3
HALO = 3
TIME_STEP = 0.08
PSEUDO_STEP = 0.3
WENO_EPS = 1e-06
ROWS = 4
MESH = pl.DeviceIdType.MESH


def turned(value, offset, axis):
    size = value.shape[axis]
    return pltpu.roll(value, (-offset) % size, axis)


def face_sides(diff, second, second_next, third, third_before, third_after, one, two, three):
    p12 = one * two
    p13 = one * three
    p23 = two * three
    p12 = p12 * p12
    p13 = p13 * p13
    p23 = p23 * p23
    u = p23 * (third_before - third)
    v = p12 * (third - third_after)
    both = u + v
    both = both + both
    shared = (p12 + p23) + 6.0 * p13
    minus = (both + v) * pl.reciprocal(shared + (p12 + p12), approx=True)
    plus = (both + u) * pl.reciprocal(shared + (p23 + p23), approx=True)
    diff6 = 6.0 * diff
    ends = second + second_next
    return diff6 + (ends + second_next) + minus, diff6 - (ends + second) - plus


def smoothness(second, third):
    t = third * third
    m = third * second
    a = (4.0 / 3.0) * t + (second * second + WENO_EPS)
    two = a + m
    three = a - m
    tm = t + m
    return two + (tm + tm), two, three


def part_of_gradient(minus, plus, sign):
    side = jnp.maximum(jnp.maximum(sign * minus, -(sign * plus)), 0.0)
    return side * side


def periodic_part(block, sign, axis):
    diff = block - turned(block, -1, axis)
    second = diff - turned(diff, -1, axis)
    second_next = turned(second, 1, axis)
    third = second_next - second
    one_next, two, three_before = smoothness(second, third)
    minus, plus = face_sides(
        diff, second, second_next, third, turned(third, -1, axis), turned(third, 1, axis),
        turned(one_next, -1, axis), two, turned(three_before, 1, axis),
    )
    return part_of_gradient(minus, turned(plus, 1, axis), sign)


def leading_part(window, sign):
    n = sign.shape[0]
    diff = window[1:] - window[:-1]
    second = diff[1:] - diff[:-1]
    third = second[1:] - second[:-1]
    one_next, two, three_before = smoothness(second[:-1], third)
    minus, plus = face_sides(
        diff[2 : n + 3], second[1 : n + 2], second[2 : n + 3], third[1 : n + 2], third[0 : n + 1], third[2 : n + 3],
        one_next[0 : n + 1], two[1 : n + 2], three_before[2 : n + 3],
    )
    return part_of_gradient(minus[:n], plus[1:], sign)


def grow(low, sec, value):
    return jnp.minimum(low, value), jnp.minimum(sec, jnp.maximum(low, value))


def merge(left, right):
    low = jnp.minimum(left[0], right[0])
    sec = jnp.minimum(jnp.maximum(left[0], right[0]), jnp.minimum(left[1], right[1]))
    return low, sec


def projected(level, low, sec):
    return 0.5 * (level - jnp.where(level == low, sec, low))


def kernel(
    sizes, ids_ref, table_ref, mob_ref, out_ref,
    ids, mob, colour, flow, lev, sig, ranks, got_one, half, got_two, final,
    in_send, in_recv, halo_send, halo_recv, set_send, set_recv,
):
    count, near, far, slab_devices, depth = sizes
    group, part, slab = lax.axis_index("groups"), lax.axis_index("set"), lax.axis_index("gy")
    up = lax.rem(slab + slab_devices - 1, slab_devices)
    down = lax.rem(slab + 1, slab_devices)
    low_bit = lax.rem(part, 2)
    sibling = part + 1 - 2 * low_bit
    cross = lax.rem(part + 2, 4)
    to_up, to_down = (group, part, up), (group, part, down)
    to_sibling, to_cross = (group, sibling, slab), (group, cross, slab)

    barrier = pltpu.get_barrier_semaphore()
    for target in (to_up, to_down, to_sibling, to_cross):
        pl.semaphore_signal(barrier, inc=1, device_id=target, device_id_type=MESH)

    for y in range(near):
        ids[far + y] = ids_ref[pl.ds(y, depth, stride=near), :]
        mob[far + y] = TIME_STEP * mob_ref[pl.ds(y, depth, stride=near), :]

    pl.semaphore_wait(barrier, 4)

    def remote(src, dst, send, recv, target):
        return pltpu.make_async_remote_copy(
            src_ref=src, dst_ref=dst, send_sem=send, recv_sem=recv, device_id=target, device_id_type=MESH
        )

    starts = [
        remote(ids.at[pl.ds(far, far)], ids.at[pl.ds(far + near, far)], in_send.at[0], in_recv.at[0], to_up),
        remote(ids.at[pl.ds(near, far)], ids.at[pl.ds(0, far)], in_send.at[1], in_recv.at[1], to_down),
        remote(mob.at[pl.ds(far, HALO)], mob.at[pl.ds(far + near, HALO)], in_send.at[2], in_recv.at[2], to_up),
        remote(mob.at[pl.ds(far + near - HALO, HALO)], mob.at[pl.ds(far - HALO, HALO)], in_send.at[3], in_recv.at[3], to_down),
    ]
    for copy in starts:
        copy.start()

    def colours(first, rows):
        cells = ids[first : first + rows].reshape(rows * depth, 128)
        lane = jnp.bitwise_and(cells, 127)
        line = lax.shift_right_logical(cells, 7)

        def look(at, found):
            entry = jnp.broadcast_to(table_ref[pl.ds(at, 1), :], cells.shape)
            return jnp.where(line == at, jnp.take_along_axis(entry, lane, axis=1), found)

        lines = table_ref.shape[0]
        found = jnp.zeros_like(cells)
        if lines <= 8:
            for at in range(lines):
                found = look(at, found)
        else:
            found = lax.fori_loop(0, lines, look, found)
        colour[first : first + rows] = found.reshape(rows, depth, 128)

    colours(far, near)
    for copy in starts:
        copy.wait()
    colours(0, far)
    colours(far + near, far)

    wide = near + 2 * HALO

    def first_row(y, _):
        def marks(at):
            c = colour[at]
            bit = lax.shift_left(jnp.ones_like(c), 4 * jnp.bitwise_and(c, 7))
            return jnp.where(c < 8, bit, 0), jnp.where(c < 8, 0, bit)

        here = colour[y + 1]
        words = []
        for before, mine, after in zip(marks(y), marks(y + 1), marks(y + 2)):
            words.append(
                before + after + turned(mine, 1, 0) + turned(mine, -1, 0) + turned(mine, 1, 1) + turned(mine, -1, 1)
            )
        pace = mob[y + 1]
        low = sec = None
        for k in range(SETS):
            n = jnp.bitwise_and(lax.shift_right_logical(words[k // 8], 4 * (k % 8)), 7).astype(jnp.float32)
            value = jnp.where(here == k, pace * (6.0 - n) - 0.5, 0.5 - pace * n)
            flow[k, y] = value
            if k == 0:
                low, sec = value, jnp.full_like(value, jnp.inf)
            else:
                low, sec = grow(low, sec, value)
        for i in range(count):
            lev[0, i, y] = projected(flow[part * count + i, y], low, sec)
        return 0

    lax.fori_loop(0, wide, first_row, 0)

    def set_signs():
        def of(i, _):
            def rows(b, _):
                level = lev[0, i, pl.ds(HALO + b * ROWS, ROWS)]
                sig[i, pl.ds(b * ROWS, ROWS)] = level * lax.rsqrt(level * level + 1.0)
                return 0

            return lax.fori_loop(0, near // ROWS, rows, 0)

        lax.fori_loop(0, count, of, 0)

    set_signs()

    def halo_copies(at, k):
        return (
            remote(
                lev.at[at, k, pl.ds(HALO, HALO)], lev.at[at, k, pl.ds(HALO + near, HALO)],
                halo_send.at[at, 0, k], halo_recv.at[at, 0, k], to_up,
            ),
            remote(
                lev.at[at, k, pl.ds(near, HALO)], lev.at[at, k, pl.ds(0, HALO)],
                halo_send.at[at, 1, k], halo_recv.at[at, 1, k], to_down,
            ),
        )

    def send_halo(at, k):
        for copy in halo_copies(at, k):
            copy.start()

    def wait_halo(at, k):
        for copy in halo_copies(at, k):
            copy.wait()

    def sweep(at, wait, last):
        def of(k, _):
            if wait:
                wait_halo(at, k)

            def rows(b, _):
                first = b * ROWS
                window = lev[at, k, pl.ds(first, ROWS + 2 * HALO)]
                signum = sig[k, pl.ds(first, ROWS)]
                sign = jnp.where(signum > 0.0, 1.0, -1.0)
                block = window[HALO : HALO + ROWS]
                gradient = periodic_part(block, sign, 1) + leading_part(window, sign) + periodic_part(block, sign, 2)
                new = block - PSEUDO_STEP * signum * (jnp.sqrt(gradient) * (1.0 / 6.0) - 1.0)
                if last:
                    for y in range(ROWS):
                        out_ref[k, pl.ds(first + y, depth, stride=near), :] = new[y]
                else:
                    lev[1 - at, k, pl.ds(HALO + first, ROWS)] = new
                return 0

            lax.fori_loop(0, near // ROWS, rows, 0)
            if not last:
                send_halo(1 - at, k)
            return 0

        lax.fori_loop(0, count, of, 0)

    sweep(0, False, False)
    sweep(1, True, False)
    sweep(0, True, False)

    for k in range(count):
        wait_halo(1, k)

    def flow_row(y, _):
        pace = mob[far + y]
        low = sec = None
        for k in range(count):
            mine = lev[1, k, HALO + y]
            laplace = turned(mine, 1, 0) + turned(mine, -1, 0) + lev[1, k, HALO + y - 1] + lev[1, k, HALO + y + 1]
            laplace = laplace + turned(mine, 1, 1) + turned(mine, -1, 1) - 6.0 * mine
            value = mine + pace * laplace
            lev[0, k, HALO + y] = value
            if k == 0:
                low, sec = value, jnp.full_like(value, jnp.inf)
            else:
                low, sec = grow(low, sec, value)
        ranks[y, 0] = low
        ranks[y, 1] = sec
        return 0

    lax.fori_loop(0, near, flow_row, 0)

    some = near // 2
    own = low_bit * some
    other = some - own
    first = remote(ranks.at[pl.ds(other, some)], got_one, set_send.at[0], set_recv.at[0], to_sibling)
    first.start()
    first.wait()

    def merge_one(y, _):
        low, sec = merge((ranks[own + y, 0], ranks[own + y, 1]), (got_one[y, 0], got_one[y, 1]))
        half[y, 0] = low
        half[y, 1] = sec
        return 0

    lax.fori_loop(0, some, merge_one, 0)
    second = remote(half, got_two, set_send.at[1], set_recv.at[1], to_cross)
    second.start()
    second.wait()

    def merge_two(y, _):
        low, sec = merge((half[y, 0], half[y, 1]), (got_two[y, 0], got_two[y, 1]))
        final[own + y, 0] = low
        final[own + y, 1] = sec
        return 0

    lax.fori_loop(0, some, merge_two, 0)
    third = remote(final.at[pl.ds(own, some)], final.at[pl.ds(own, some)], set_send.at[2], set_recv.at[2], to_sibling)
    third.start()
    third.wait()

    def project_of(k, _):
        def row(y, _):
            lev[0, k, HALO + y] = projected(lev[0, k, HALO + y], final[y, 0], final[y, 1])
            return 0

        lax.fori_loop(0, near, row, 0)
        send_halo(0, k)
        return 0

    lax.fori_loop(0, count, project_of, 0)
    set_signs()

    sweep(0, True, False)
    sweep(1, True, False)
    sweep(0, True, True)


def solution(mesh):
    slab_devices = mesh.shape["gy"]
    count = SETS // mesh.shape["set"]

    def shards(grain_ids, colouring, mobility):
        depth, near, width = grain_ids.shape
        far = HALO + 1
        wide = near + 2 * HALO
        tile = (depth, width)
        out = pl.pallas_call(
            functools.partial(kernel, (count, near, far, slab_devices, depth)),
            out_shape=jax.ShapeDtypeStruct((count, depth * near, width), jnp.float32),
            in_specs=[pl.BlockSpec(memory_space=pltpu.VMEM)] * 3,
            out_specs=pl.BlockSpec(memory_space=pltpu.VMEM),
            scratch_shapes=[
                pltpu.VMEM((near + 2 * far,) + tile, jnp.int32),
                pltpu.VMEM((near + 2 * far,) + tile, jnp.float32),
                pltpu.VMEM((near + 2 * far,) + tile, jnp.int32),
                pltpu.VMEM((SETS, wide) + tile, jnp.float32),
                pltpu.VMEM((2, count, wide) + tile, jnp.float32),
                pltpu.VMEM((count, near) + tile, jnp.float32),
                pltpu.VMEM((near, 2) + tile, jnp.float32),
                pltpu.VMEM((near // 2, 2) + tile, jnp.float32),
                pltpu.VMEM((near // 2, 2) + tile, jnp.float32),
                pltpu.VMEM((near // 2, 2) + tile, jnp.float32),
                pltpu.VMEM((near, 2) + tile, jnp.float32),
                pltpu.SemaphoreType.DMA((4,)),
                pltpu.SemaphoreType.DMA((4,)),
                pltpu.SemaphoreType.DMA((2, 2, count)),
                pltpu.SemaphoreType.DMA((2, 2, count)),
                pltpu.SemaphoreType.DMA((3,)),
                pltpu.SemaphoreType.DMA((3,)),
            ],
            compiler_params=pltpu.CompilerParams(
                collective_id=0, has_side_effects=True, vmem_limit_bytes=32 * 1024 * 1024
            ),
        )(
            grain_ids.reshape(depth * near, width),
            colouring.reshape(-1, width),
            mobility.reshape(depth * near, width),
        )
        return out.reshape(count, depth, near, width)

    return jax.shard_map(
        shards,
        mesh=mesh,
        in_specs=(P("groups", "gy", None), P("groups"), P("groups", "gy", None)),
        out_specs=P(("groups", "set"), None, "gy", None),
        check_vma=False,
    )
```

time: 185 us -> 67.1 us (0.36)
  local copies, waits for them, and re-layouts: 72.5 us -> 3.07 us
  Pallas kernels: 0 us -> 63.8 us
  starting transfers between devices: 32.2 us -> 0 us
  other arithmetic: 31.1 us -> 0 us
  waiting for transfers between devices: 24.9 us -> 0 us
  blocking collectives: 23.3 us -> 0 us
    gather x1 -> x0, local copies, waits for them, and re-layouts: 65.3 us -> none  [shards(): colour_cell = jnp.take(colouring, grain_ids)]
    pallas_call x0 -> x1, Pallas kernels: none -> 63.8 us  [shards(): pl.pallas_call(functools.partial(kernel, (count, near, far, slab_devices,...]
    ppermute x16 -> x0, starting transfers between devices: 32.2 us -> none  [the longest x8 29.7 us: padded_2(): after = lax.ppermute(leading, axis, down)]
    sub x6 -> x0, other arithmetic: 29.2 us -> none  [settle(): return center - PSEUDO_STEP * signum * (jnp.sqrt(gradient) - 1.0)]
    ppermute x16 -> x0, waiting for transfers between devices: 24.9 us -> none  [the longest x8 23.1 us: padded_2(): before = lax.ppermute(last, axis, up)]
    all_gather x4 -> x0, blocking collectives: 23.3 us -> none  [joined(): everything = jax.tree.map(lambda part: lax.all_gather(part, axis), shard)]
    slice x88 -> x0, local copies, waits for them, and re-layouts: 6.36 us -> none  [the longest x72 5.55 us: rolled(): return jnp.roll(field, -offset, along_axis)]
    unnamed x6 -> x7, local copies, waits for them, and re-layouts: 0.81 us -> 3.07 us
  transfers between devices with their start and end apart: 16 -> 0, of which waited for: 10 -> 0; matrix products, arithmetic and copies ran while one was open for 0% -> 0% of each run, Pallas kernels for 0% -> 0%
where the time goes in v1:
time: 67.1 us; the launch traced here: 66.9 us
  Pallas kernels  63.8 us (95%)
  local copies, waits for them, and re-layouts  3.07 us (5%)
    pallas_call x1, Pallas kernels, shards(): pl.pallas_call(functools.partial(kernel, (count, near, far, slab_devices,...  63.8 us
    unnamed x7, local copies, waits for them, and re-layouts  3.07 us

profile of v1, /device:TPU:0, one launch (start us, length us, event | category | flops | bytes accessed | tf_op | source)
XLA Modules:
  0.0 66.9 jit_solution(10664768368966743645)
XLA Ops:
  0.0 0.0 copy-start.2
  0.0 0.7 %copy-done.2 = s32[1024]{0:T(1024)S(1)} copy-done((s32[1024]{0:T(1024)S(1)}, s32[1024]{0:T(1024)}, u32[]{:S(2)}) %copy-start.2) | copy-done | bytes 4120
  0.7 0.0 copy-start
  0.7 0.8 %copy-done = s32[8,16,128]{2,1,0:T(8,128)S(1)} copy-done((s32[8,16,128]{2,1,0:T(8,128)S(1)}, s32[8,16,128]{2,1,0:T(8,128)}, u32[]{:S(2)}) %copy-start) | copy-done | bytes 65560
  1.5 0.0 copy-start.1
  1.5 0.8 %copy-done.1 = f32[8,16,128]{2,1,0:T(8,128)S(1)} copy-done((f32[8,16,128]{2,1,0:T(8,128)S(1)}, f32[8,16,128]{2,1,0:T(8,128)}, u32[]{:S(2)}) %copy-start.1) | copy-done | bytes 65560
  2.4 63.8 %shard_map.37 = f32[4,128,128]{2,1,0:T(8,128)S(1)} custom-call(s32[128,128]{1,0:T(8,128)S(1)} %bitcast.5, s32[8,128]{1,0:T(8,128)S(1)} %bitcast.7, f32[128,128]{1,0:T(8,128)S(1)} %bitcast.6), custom_call_target="tpu_custom_call" | custom-call | tf_op jit(solution)/shard_map/pallas_call | solution.py:333
  66.2 0.7 %copy.5 = f32[4,8,16,128]{3,2,1,0:T(8,128)} copy(f32[4,8,16,128]{3,2,1,0:T(8,128)S(1)} %bitcast.4) | data formatting | bytes 524288
Async XLA Ops:
  0.0 0.7 %copy-start.2 = (s32[1024]{0:T(1024)S(1)}, s32[1024]{0:T(1024)}, u32[]{:S(2)}) copy-start(s32[1024]{0:T(1024)} %param.4) | copy-start | bytes 12292
  0.7 0.8 %copy-start = (s32[8,16,128]{2,1,0:T(8,128)S(1)}, s32[8,16,128]{2,1,0:T(8,128)}, u32[]{:S(2)}) copy-start(s32[8,16,128]{2,1,0:T(8,128)} %param.3) | copy-start | bytes 196612
  1.5 0.8 %copy-start.1 = (f32[8,16,128]{2,1,0:T(8,128)S(1)}, f32[8,16,128]{2,1,0:T(8,128)}, u32[]{:S(2)}) copy-start(f32[8,16,128]{2,1,0:T(8,128)} %param.5) | copy-start | bytes 196612

commit v2 on v1

v2 whole, which is shorter than its diff:
```python
import functools

import jax
import jax.numpy as jnp
from jax import lax
from jax.experimental import pallas as pl
from jax.experimental.pallas import tpu as pltpu
from jax.sharding import PartitionSpec as P

SETS = 16
REINIT = 3
HALO = 3
TIME_STEP = 0.08
PSEUDO_STEP = 0.3
WENO_EPS = 1e-06
WIDER = 2 * HALO
MESH = pl.DeviceIdType.MESH


def turned(value, offset, axis):
    size = value.shape[axis]
    return pltpu.roll(value, (-offset) % size, axis)


def face_sides(diff, second, second_next, third, third_before, third_after, one, two, three):
    p12 = one * two
    p13 = one * three
    p23 = two * three
    p12 = p12 * p12
    p13 = p13 * p13
    p23 = p23 * p23
    u = p23 * (third_before - third)
    v = p12 * (third - third_after)
    both = u + v
    both = both + both
    shared = (p12 + p23) + 6.0 * p13
    minus = (both + v) * pl.reciprocal(shared + (p12 + p12), approx=True)
    plus = (both + u) * pl.reciprocal(shared + (p23 + p23), approx=True)
    diff6 = 6.0 * diff
    ends = second + second_next
    return diff6 + (ends + second_next) + minus, diff6 - (ends + second) - plus


def smoothness(second, third):
    t = third * third
    m = third * second
    a = (4.0 / 3.0) * t + (second * second + WENO_EPS)
    two = a + m
    three = a - m
    tm = t + m
    return two + (tm + tm), two, three


def part_of_gradient(minus, plus, sign):
    side = jnp.maximum(jnp.maximum(sign * minus, -(sign * plus)), 0.0)
    return side * side


def periodic_part(block, sign, axis):
    diff = block - turned(block, -1, axis)
    second = diff - turned(diff, -1, axis)
    second_next = turned(second, 1, axis)
    third = second_next - second
    third_before, third_after = turned(third, -1, axis), turned(third, 1, axis)
    if axis == 1:
        one_next, two, three_before = smoothness(second, third)
        one, three = turned(one_next, -1, axis), turned(three_before, 1, axis)
    else:
        here = second * second + WENO_EPS
        one = third_before * ((4.0 / 3.0) * third_before + second) + here
        two = third * ((4.0 / 3.0) * third + second) + here
        three = third_after * ((4.0 / 3.0) * third_after - second_next) + (second_next * second_next + WENO_EPS)
    minus, plus = face_sides(diff, second, second_next, third, third_before, third_after, one, two, three)
    return part_of_gradient(minus, turned(plus, 1, axis), sign)


def leading_part(window, sign):
    n = sign.shape[0]
    diff = window[1:] - window[:-1]
    second = diff[1:] - diff[:-1]
    third = second[1:] - second[:-1]
    one_next, two, three_before = smoothness(second[:-1], third)
    minus, plus = face_sides(
        diff[2 : n + 3], second[1 : n + 2], second[2 : n + 3], third[1 : n + 2], third[0 : n + 1], third[2 : n + 3],
        one_next[0 : n + 1], two[1 : n + 2], three_before[2 : n + 3],
    )
    return part_of_gradient(minus[:n], plus[1:], sign)


def grow(low, sec, value):
    return jnp.minimum(low, value), jnp.minimum(sec, jnp.maximum(low, value))


def merge(left, right):
    low = jnp.minimum(left[0], right[0])
    sec = jnp.minimum(jnp.maximum(left[0], right[0]), jnp.minimum(left[1], right[1]))
    return low, sec


def projected(level, low, sec):
    return 0.5 * (level - jnp.where(level == low, sec, low))


def kernel(
    sizes, ids_ref, table_ref, mob_ref, out_ref,
    ids, mob, colour, flow, lev, sig, ranks, got_one, half, got_two, final,
    ids_in, mob_in, table, load_sem, in_send, in_recv, halo_send, halo_recv, set_send, set_recv,
):
    count, near, far, slab_devices, depth = sizes
    group, part, slab = lax.axis_index("groups"), lax.axis_index("set"), lax.axis_index("gy")
    up = lax.rem(slab + slab_devices - 1, slab_devices)
    down = lax.rem(slab + 1, slab_devices)
    low_bit = lax.rem(part, 2)
    sibling = part + 1 - 2 * low_bit
    cross = lax.rem(part + 2, 4)
    to_up, to_down = (group, part, up), (group, part, down)
    to_sibling, to_cross = (group, sibling, slab), (group, cross, slab)

    barrier = pltpu.get_barrier_semaphore()
    for target in (to_up, to_down, to_sibling, to_cross):
        pl.semaphore_signal(barrier, inc=1, device_id=target, device_id_type=MESH)

    loads = [
        pltpu.make_async_copy(ids_ref, ids_in, load_sem.at[0]),
        pltpu.make_async_copy(mob_ref, mob_in, load_sem.at[1]),
        pltpu.make_async_copy(table_ref, table, load_sem.at[2]),
    ]
    for copy in loads:
        copy.start()
    for copy in loads:
        copy.wait()
    for y in range(near):
        ids[far + y] = ids_in[pl.ds(y, depth, stride=near), :]
        mob[far + y] = TIME_STEP * mob_in[pl.ds(y, depth, stride=near), :]

    pl.semaphore_wait(barrier, 4)

    def remote(src, dst, send, recv, target):
        return pltpu.make_async_remote_copy(
            src_ref=src, dst_ref=dst, send_sem=send, recv_sem=recv, device_id=target, device_id_type=MESH
        )

    starts = [
        remote(ids.at[pl.ds(far, far)], ids.at[pl.ds(far + near, far)], in_send.at[0], in_recv.at[0], to_up),
        remote(ids.at[pl.ds(near, far)], ids.at[pl.ds(0, far)], in_send.at[1], in_recv.at[1], to_down),
        remote(mob.at[pl.ds(far, WIDER)], mob.at[pl.ds(far + near, WIDER)], in_send.at[2], in_recv.at[2], to_up),
        remote(mob.at[pl.ds(far + near - WIDER, WIDER)], mob.at[pl.ds(far - WIDER, WIDER)], in_send.at[3], in_recv.at[3], to_down),
    ]
    for copy in starts:
        copy.start()

    def colours(first, rows):
        cells = ids[first : first + rows].reshape(rows * depth, 128)
        lane = jnp.bitwise_and(cells, 127)
        line = lax.shift_right_logical(cells, 7)

        def look(at, found):
            entry = jnp.broadcast_to(table[pl.ds(at, 1), :], cells.shape)
            return jnp.where(line == at, jnp.take_along_axis(entry, lane, axis=1), found)

        lines = table.shape[0]
        found = jnp.zeros_like(cells)
        if lines <= 8:
            for at in range(lines):
                found = look(at, found)
        else:
            found = lax.fori_loop(0, lines, look, found)
        colour[first : first + rows] = found.reshape(rows, depth, 128)

    colours(far, near)

    wide = near + 2 * WIDER

    inner = (near - 2) // 2

    def settle(i, rows, value, low, sec):
        level = projected(value, low, sec)
        lev[0, i, pl.ds(rows.start + 1, rows.size)] = level
        sig[i, rows] = level * lax.rsqrt(level * level + 1.0)

    def first_rows(y, n):
        c = colour[pl.ds(y, n + 2)]
        bit = lax.shift_left(jnp.ones_like(c), 4 * jnp.bitwise_and(c, 7))
        here = c[1 : n + 1]
        words = []
        for marks in (jnp.where(c < 8, bit, 0), jnp.where(c < 8, 0, bit)):
            mine = marks[1 : n + 1]
            words.append(
                marks[:n] + marks[2:] + turned(mine, 1, 1) + turned(mine, -1, 1) + turned(mine, 1, 2) + turned(mine, -1, 2)
            )
        pace = mob[pl.ds(y + 1, n)]
        low = sec = None
        for k in range(SETS):
            faces = jnp.bitwise_and(lax.shift_right_logical(words[k // 8], 4 * (k % 8)), 7).astype(jnp.float32)
            value = jnp.where(here == k, pace * (6.0 - faces) - 0.5, 0.5 - pace * faces)
            flow[k, pl.ds(y, n)] = value
            if k == 0:
                low, sec = value, jnp.full_like(value, jnp.inf)
            else:
                low, sec = grow(low, sec, value)
        for i in range(count):
            settle(i, pl.ds(y, n), flow[part * count + i, pl.ds(y, n)], low, sec)

    def inner_rows(of):
        def block(b, _):
            of(far + b * inner, inner)
            return 0

        lax.fori_loop(0, 2, block, 0)

    def outer_rows(of):
        def block(b, _):
            of(b * (wide - far), far)
            return 0

        lax.fori_loop(0, 2, block, 0)

    inner_rows(first_rows)
    for copy in starts:
        copy.wait_recv()
    colours(0, far)
    colours(far + near, far)
    outer_rows(first_rows)

    def halo_copies(message, at, k, rows):
        return (
            remote(
                lev.at[at, k, pl.ds(far, rows)], lev.at[at, k, pl.ds(far + near, rows)],
                halo_send.at[message, 0, k], halo_recv.at[message, 0, k], to_up,
            ),
            remote(
                lev.at[at, k, pl.ds(far + near - rows, rows)], lev.at[at, k, pl.ds(far - rows, rows)],
                halo_send.at[message, 1, k], halo_recv.at[message, 1, k], to_down,
            ),
        )

    def send_halo(*message):
        for copy in halo_copies(*message):
            copy.start()

    def wait_halo(*message):
        for copy in halo_copies(*message):
            copy.wait_recv()

    def wait_sent(*message):
        for copy in halo_copies(*message):
            copy.wait_send()

    def sweep(at, to, k, margin):
        rows = near + 2 * margin
        window = lev[at, k, pl.ds(far - margin - HALO, rows + 2 * HALO)]
        signum = sig[k, pl.ds(WIDER - margin, rows)]
        sign = jnp.where(signum > 0.0, 1.0, -1.0)
        block = window[HALO : HALO + rows]
        gradient = periodic_part(block, sign, 1) + leading_part(window, sign) + periodic_part(block, sign, 2)
        new = block - PSEUDO_STEP * signum * (jnp.sqrt(gradient) * (1.0 / 6.0) - 1.0)
        if to is None:
            for y in range(near):
                out_ref[k, pl.ds(y, depth, stride=near), :] = new[y]
        else:
            lev[to, k, pl.ds(far - margin, rows)] = new

    def step_one(k, _):
        sweep(0, 1, k, HALO)
        sweep(1, 2, k, 0)
        send_halo(0, 2, k, HALO)
        return 0

    def step_one_end(k, _):
        wait_halo(0, 2, k, HALO)
        sweep(2, 1, k, 0)
        send_halo(1, 1, k, far)
        return 0

    lax.fori_loop(0, count, step_one, 0)
    lax.fori_loop(0, count, step_one_end, 0)

    def flow_rows(y, n):
        pace = mob[pl.ds(y + 1, n)]
        low = sec = None
        for k in range(count):
            window = lev[1, k, pl.ds(y, n + 2)]
            mine = window[1 : n + 1]
            laplace = turned(mine, 1, 1) + turned(mine, -1, 1) + window[:n] + window[2:]
            laplace = laplace + turned(mine, 1, 2) + turned(mine, -1, 2) - 6.0 * mine
            value = mine + pace * laplace
            lev[0, k, pl.ds(y + 1, n)] = value
            if k == 0:
                low, sec = value, jnp.full_like(value, jnp.inf)
            else:
                low, sec = grow(low, sec, value)
        ranks[0, pl.ds(y, n)] = low
        ranks[1, pl.ds(y, n)] = sec

    inner_rows(flow_rows)
    for k in range(count):
        wait_halo(1, 1, k, far)
    outer_rows(flow_rows)

    some = wide // 2
    own = low_bit * some
    other = some - own
    mine, theirs = pl.ds(own, some), pl.ds(other, some)
    first = remote(ranks.at[:, theirs], got_one, set_send.at[0], set_recv.at[0], to_sibling)
    first.start()
    first.wait_recv()
    half[0], half[1] = merge((ranks[0, mine], ranks[1, mine]), (got_one[0], got_one[1]))
    second = remote(half, got_two, set_send.at[1], set_recv.at[1], to_cross)
    second.start()
    second.wait_recv()

    final[0, mine], final[1, mine] = merge((half[0], half[1]), (got_two[0], got_two[1]))
    third = remote(final.at[:, mine], final.at[:, mine], set_send.at[2], set_recv.at[2], to_sibling)
    third.start()
    third.wait_recv()

    def step_two(k, _):
        wait_sent(1, 1, k, far)
        settle(k, pl.ds(0, wide), lev[0, k, pl.ds(1, wide)], final[0], final[1])
        sweep(0, 1, k, HALO)
        wait_sent(0, 2, k, HALO)
        sweep(1, 2, k, 0)
        send_halo(2, 2, k, HALO)
        return 0

    def step_two_end(k, _):
        wait_halo(2, 2, k, HALO)
        sweep(2, None, k, 0)
        wait_sent(2, 2, k, HALO)
        return 0

    lax.fori_loop(0, count, step_two, 0)
    lax.fori_loop(0, count, step_two_end, 0)
    for copy in starts + [first, second, third]:
        copy.wait_send()


def solution(mesh):
    slab_devices = mesh.shape["gy"]
    count = SETS // mesh.shape["set"]

    def shards(grain_ids, colouring, mobility):
        depth, near, width = grain_ids.shape
        far = WIDER + 1
        wide = near + 2 * WIDER
        tile = (depth, width)
        out = pl.pallas_call(
            functools.partial(kernel, (count, near, far, slab_devices, depth)),
            out_shape=jax.ShapeDtypeStruct((count, depth * near, width), jnp.float32),
            in_specs=[pl.BlockSpec(memory_space=pltpu.HBM)] * 3,
            out_specs=pl.BlockSpec(memory_space=pltpu.VMEM),
            scratch_shapes=[
                pltpu.VMEM((near + 2 * far,) + tile, jnp.int32),
                pltpu.VMEM((near + 2 * far,) + tile, jnp.float32),
                pltpu.VMEM((near + 2 * far,) + tile, jnp.int32),
                pltpu.VMEM((SETS, wide) + tile, jnp.float32),
                pltpu.VMEM((3, count, near + 2 * far) + tile, jnp.float32),
                pltpu.VMEM((count, wide) + tile, jnp.float32),
                pltpu.VMEM((2, wide) + tile, jnp.float32),
                pltpu.VMEM((2, wide // 2) + tile, jnp.float32),
                pltpu.VMEM((2, wide // 2) + tile, jnp.float32),
                pltpu.VMEM((2, wide // 2) + tile, jnp.float32),
                pltpu.VMEM((2, wide) + tile, jnp.float32),
                pltpu.VMEM((depth * near, width), jnp.int32),
                pltpu.VMEM((depth * near, width), jnp.float32),
                pltpu.VMEM((colouring.size // width, width), jnp.int32),
                pltpu.SemaphoreType.DMA((3,)),
                pltpu.SemaphoreType.DMA((4,)),
                pltpu.SemaphoreType.DMA((4,)),
                pltpu.SemaphoreType.DMA((3, 2, count)),
                pltpu.SemaphoreType.DMA((3, 2, count)),
                pltpu.SemaphoreType.DMA((3,)),
                pltpu.SemaphoreType.DMA((3,)),
            ],
            compiler_params=pltpu.CompilerParams(
                collective_id=0, has_side_effects=True
            ),
        )(
            grain_ids.reshape(depth * near, width),
            colouring.reshape(-1, width),
            mobility.reshape(depth * near, width),
        )
        return out.reshape(count, depth, near, width)

    return jax.shard_map(
        shards,
        mesh=mesh,
        in_specs=(P("groups", "gy", None), P("groups"), P("groups", "gy", None)),
        out_specs=P(("groups", "set"), None, "gy", None),
        check_vma=False,
    )
```

time: 67.1 us -> 44.5 us (0.66)
  Pallas kernels: 63.8 us -> 42.6 us
  local copies, waits for them, and re-layouts: 3.07 us -> 1.67 us
    pallas_call x1, Pallas kernels: 63.8 us -> 42.6 us  [shards(): pl.pallas_call(functools.partial(kernel, (count, near, far, slab_devices,...]
    unnamed x7 -> x1, local copies, waits for them, and re-layouts: 3.07 us -> 1.67 us
where the time goes in v2:
time: 44.5 us; the launch traced here: 44.3 us
  Pallas kernels  42.6 us (96%)
  local copies, waits for them, and re-layouts  1.67 us (4%)
    pallas_call x1, Pallas kernels, shards(): pl.pallas_call(functools.partial(kernel, (count, near, far, slab_devices,...  42.6 us
    unnamed x1, local copies, waits for them, and re-layouts  1.67 us

profile of v2, /device:TPU:0, one launch (start us, length us, event | category | flops | bytes accessed | tf_op | source)
XLA Modules:
  0.0 44.3 jit_solution(3344874563065664802)
XLA Ops:
  0.0 42.6 %shard_map.37 = f32[4,128,128]{2,1,0:T(8,128)} custom-call(s32[128,128]{1,0:T(8,128)} %bitcast.5, s32[8,128]{1,0:T(8,128)} %bitcast.7, f32[128,128]{1,0:T(8,128)} %bitcast.6), custom_call_target="tpu_custom_call" | custom-call | tf_op jit(solution)/shard_map/pallas_call | solution.py:347
  42.6 1.7 %copy.5 = f32[4,8,16,128]{3,2,1,0:T(8,128)} copy(f32[4,8,16,128]{3,2,1,0:T(8,128)} %bitcast.4) | data formatting | bytes 524288

commit v3 on v2

--- a/solution.py
+++ b/solution.py
@@ -292,27 +292,45 @@
         ranks[0, pl.ds(y, n)] = low
         ranks[1, pl.ds(y, n)] = sec
 
+    def join(turn, n, start):
+        mine, theirs = pl.ds(start(low_bit), n), pl.ds(start(1 - low_bit), n)
+        here = pl.ds(0, n)
+        first = remote(
+            ranks.at[:, theirs], got_one.at[turn, :, here], set_send.at[turn, 0], set_recv.at[turn, 0], to_sibling
+        )
+        first.start()
+        yield
+        first.wait_recv()
+        half[turn, 0, here], half[turn, 1, here] = merge(
+            (ranks[0, mine], ranks[1, mine]), (got_one[turn, 0, here], got_one[turn, 1, here])
+        )
+        second = remote(
+            half.at[turn, :, here], got_two.at[turn, :, here], set_send.at[turn, 1], set_recv.at[turn, 1], to_cross
+        )
+        second.start()
+        yield
+        second.wait_recv()
+        final[0, mine], final[1, mine] = merge(
+            (half[turn, 0, here], half[turn, 1, here]), (got_two[turn, 0, here], got_two[turn, 1, here])
+        )
+        third = remote(final.at[:, mine], final.at[:, mine], set_send.at[turn, 2], set_recv.at[turn, 2], to_sibling)
+        third.start()
+        yield
+        third.wait_recv()
+        joins.extend([first, second, third])
+        yield
+
     inner_rows(flow_rows)
+    joins = []
+    inner_join = join(0, inner, lambda b: far + b * inner)
+    outer_join = join(1, far, lambda b: b * (wide - far))
+    next(inner_join)
+    next(inner_join)
     for k in range(count):
         wait_halo(1, 1, k, far)
     outer_rows(flow_rows)
-
-    some = wide // 2
-    own = low_bit * some
-    other = some - own
-    mine, theirs = pl.ds(own, some), pl.ds(other, some)
-    first = remote(ranks.at[:, theirs], got_one, set_send.at[0], set_recv.at[0], to_sibling)
-    first.start()
-    first.wait_recv()
-    half[0], half[1] = merge((ranks[0, mine], ranks[1, mine]), (got_one[0], got_one[1]))
-    second = remote(half, got_two, set_send.at[1], set_recv.at[1], to_cross)
-    second.start()
-    second.wait_recv()
-
-    final[0, mine], final[1, mine] = merge((half[0], half[1]), (got_two[0], got_two[1]))
-    third = remote(final.at[:, mine], final.at[:, mine], set_send.at[2], set_recv.at[2], to_sibling)
-    third.start()
-    third.wait_recv()
+    for step in (outer_join, inner_join, outer_join, outer_join, inner_join, outer_join):
+        next(step)
 
     def step_two(k, _):
         wait_sent(1, 1, k, far)
@@ -331,7 +349,7 @@
 
     lax.fori_loop(0, count, step_two, 0)
     lax.fori_loop(0, count, step_two_end, 0)
-    for copy in starts + [first, second, third]:
+    for copy in starts + joins:
         copy.wait_send()
 
 
@@ -357,9 +375,9 @@
                 pltpu.VMEM((3, count, near + 2 * far) + tile, jnp.float32),
                 pltpu.VMEM((count, wide) + tile, jnp.float32),
                 pltpu.VMEM((2, wide) + tile, jnp.float32),
-                pltpu.VMEM((2, wide // 2) + tile, jnp.float32),
-                pltpu.VMEM((2, wide // 2) + tile, jnp.float32),
-                pltpu.VMEM((2, wide // 2) + tile, jnp.float32),
+                pltpu.VMEM((2, 2, far) + tile, jnp.float32),
+                pltpu.VMEM((2, 2, far) + tile, jnp.float32),
+                pltpu.VMEM((2, 2, far) + tile, jnp.float32),
                 pltpu.VMEM((2, wide) + tile, jnp.float32),
                 pltpu.VMEM((depth * near, width), jnp.int32),
                 pltpu.VMEM((depth * near, width), jnp.float32),
@@ -369,8 +387,8 @@
                 pltpu.SemaphoreType.DMA((4,)),
                 pltpu.SemaphoreType.DMA((3, 2, count)),
                 pltpu.SemaphoreType.DMA((3, 2, count)),
-                pltpu.SemaphoreType.DMA((3,)),
-                pltpu.SemaphoreType.DMA((3,)),
+                pltpu.SemaphoreType.DMA((2, 3)),
+                pltpu.SemaphoreType.DMA((2, 3)),
             ],
             compiler_params=pltpu.CompilerParams(
                 collective_id=0, has_side_effects=True

time: 44.5 us -> 43.3 us (0.973)
  Pallas kernels: 42.6 us -> 41.4 us
    pallas_call x1, Pallas kernels: 42.6 us -> 41.4 us  [shards(): pl.pallas_call(functools.partial(kernel, (count, near, far, slab_devices,...]
where the time goes in v3:
time: 43.3 us; the launch traced here: 43.1 us
  Pallas kernels  41.4 us (96%)
  local copies, waits for them, and re-layouts  1.67 us (4%)
    pallas_call x1, Pallas kernels, shards(): pl.pallas_call(functools.partial(kernel, (count, near, far, slab_devices,...  41.4 us
    unnamed x1, local copies, waits for them, and re-layouts  1.67 us

profile of v3, /device:TPU:0, one launch (start us, length us, event | category | flops | bytes accessed | tf_op | source)
XLA Modules:
  0.0 43.1 jit_solution(7801452422856756168)
XLA Ops:
  0.0 41.4 %shard_map.37 = f32[4,128,128]{2,1,0:T(8,128)} custom-call(s32[128,128]{1,0:T(8,128)} %bitcast.5, s32[8,128]{1,0:T(8,128)} %bitcast.7, f32[128,128]{1,0:T(8,128)} %bitcast.6), custom_call_target="tpu_custom_call" | custom-call | tf_op jit(solution)/shard_map/pallas_call | solution.py:365
  41.4 1.7 %copy.5 = f32[4,8,16,128]{3,2,1,0:T(8,128)} copy(f32[4,8,16,128]{3,2,1,0:T(8,128)} %bitcast.4) | data formatting | bytes 524288
